TPU v7x, 512 devices: a whole 4x4x16 slice. The times are simulated.
512 devices in a mesh: region: 4 (over x), tile: 16 (over z), link: 8 (over y, core).
Axes of the slice: x: 4, y: 4, z: 16, core: 2. Of those that a mesh axis runs over, the one named last changes fastest.
Arguments:
- tiles: bfloat16 [4, 16, 64, 256, 256], P('region', 'tile', 'link'), may hold values from -0.1875 to 0.1875
- tile_row: int32 [4, 16, 64], P('region', 'tile', 'link'), may hold values from 0 to 15
- tile_col: int32 [4, 16, 64], P('region', 'tile', 'link'), may hold values from 0 to 7
- tile_count: int32 [4, 16, 8], P('region', 'tile', 'link'), may hold values from 1 to 8, 33 in all within a row
- linkage_tiles: bfloat16 [4, 16, 8, 256, 256], P('region', 'tile', 'link'), may hold values from -0.046875 to 0.046875
- linkage_block: int32 [4, 16, 8], P('region', 'tile', 'link'), may hold values from 0 to 7
- column_cost: float32 [131072], P(('region', 'tile', 'link')), may hold values from -6 to 6
- capacity_cost: float32 [2048], P('link'), may hold values from -6 to 6
- demand: float32 [32, 131072], P(None, ('region', 'tile', 'link')), may hold values from -6 to 6
- linkage_bound: float32 [2048], P('link'), may hold values from -6 to 6
- primal_now: float32 [32, 131072], P(None, ('region', 'tile', 'link')), may hold values from 0 to 2
- capacity_now: float32 [32, 2048], P(None, 'link'), may hold values from 0 to 2
- duals_now: float32 [32, 131072], P(None, ('region', 'tile', 'link')), may hold values from 0 to 2
- linkage_now: float32 [32, 2048], P(None, 'link'), may hold values from 0 to 2
- primal_mean: float32 [32, 131072], P(None, ('region', 'tile', 'link')), may hold values from 0 to 2
- capacity_mean: float32 [32, 2048], P(None, 'link'), may hold values from 0 to 2
- duals_mean: float32 [32, 131072], P(None, ('region', 'tile', 'link')), may hold values from 0 to 2
- linkage_mean: float32 [32, 2048], P(None, 'link'), may hold values from 0 to 2
- restart: int32 [32], replicated, may hold values from 0 to 1
- mean_count: int32 [32], replicated, may hold values from 1 to 8
- primal_step: float32 [32], replicated, may hold values from 0.1 to 0.4
- dual_step: float32 [32], replicated, may hold values from 0.1 to 0.4
Outputs:
- primal_next: float32 [32, 131072], P(None, ('region', 'tile', 'link'))
- capacity_next: float32 [32, 2048], P(None, 'link')
- duals_next: float32 [32, 131072], P(None, ('region', 'tile', 'link'))
- linkage_next: float32 [32, 2048], P(None, 'link')
- primal_average: float32 [32, 131072], P(None, ('region', 'tile', 'link'))
- capacity_average: float32 [32, 2048], P(None, 'link')
- duals_average: float32 [32, 131072], P(None, ('region', 'tile', 'link'))
- linkage_average: float32 [32, 2048], P(None, 'link')
- movement: float32 [32], replicated
Inputs may be any that keep to these rules, and one draw needn't show every extreme that they name: `tile_count`: each region and tile index has one device holding exactly 8 live slots; slots at or past a device's count are ignored. `restart`: 1 restarts a scenario from its averages.
All inputs are finite; a program needn't handle non-finite values.
Results may differ from a plain program's by a relative error of at most 0.0013.
Values may be sent and summed in bfloat16 or wider, within the bound.
A program may use at most 64 MiB of HBM per device.

v0:
```python
import jax
import jax.numpy as jnp
from jax import lax
from jax.sharding import PartitionSpec as P

HIGH = lax.Precision.HIGHEST


def on_device(
    tiles,
    tile_row,
    tile_col,
    tile_count,
    linkage_tiles,
    linkage_block,
    column_cost,
    capacity_cost,
    demand,
    linkage_bound,
    primal_now,
    capacity_now,
    duals_now,
    linkage_now,
    primal_mean,
    capacity_mean,
    duals_mean,
    linkage_mean,
    restart,
    mean_count,
    primal_step,
    dual_step,
):
    across_tile = lax.axis_size("tile")
    across_link = lax.axis_size("link")
    scenarios, tile_width = primal_now.shape
    slots = tile_row.shape[2]
    slabs = tiles.reshape(slots, tile_width, tile_width)
    row_ids = tile_row.reshape(slots)
    column_ids = tile_col.reshape(slots)
    live_count = tile_count.reshape(())
    active = jnp.arange(slots, dtype=jnp.int32) < live_count
    row_pick = (
        (row_ids[:, None] == jnp.arange(across_tile, dtype=jnp.int32)[None, :]) & active[:, None]
    ).astype(jnp.float32)
    column_pick = (
        (column_ids[:, None] == jnp.arange(across_link, dtype=jnp.int32)[None, :]) & active[:, None]
    ).astype(jnp.float32)
    linkage_slab = linkage_tiles.reshape(tile_width, tile_width)
    target = linkage_block.reshape(())
    link_pick = (jnp.arange(across_link, dtype=jnp.int32) == target).astype(jnp.float32)
    restarted = (restart == 1)[:, None]
    primal_start = jnp.where(restarted, primal_mean, primal_now)
    capacity_start = jnp.where(restarted, capacity_mean, capacity_now)
    duals_start = jnp.where(restarted, duals_mean, duals_now)
    linkage_start = jnp.where(restarted, linkage_mean, linkage_now)
    step_p = primal_step[:, None]
    step_d = dual_step[:, None]
    duals_work, demand_work = (duals_start, demand)
    capacity_work, linkage_work, cost_work, bound_work = (
        lax.all_gather(capacity_start, "link", axis=1, tiled=True),
        lax.all_gather(linkage_start, "link", axis=1, tiled=True),
        lax.all_gather(capacity_cost, "link", axis=0, tiled=True),
        lax.all_gather(linkage_bound, "link", axis=0, tiled=True),
    )
    primal, capacity, duals, linkage = (primal_start, capacity_work, duals_work, linkage_work)
    history = []
    for sweep in range(2):
        transpose_spread = lax.all_gather(duals.astype(jnp.bfloat16), "tile", axis=1, tiled=True)
        picked = jnp.take(
            transpose_spread.reshape(scenarios, across_tile, tile_width), row_ids, axis=1
        )
        terms = jnp.einsum("ski,kij->skj", picked, slabs, preferred_element_type=jnp.float32)
        partial_value = jnp.einsum("skj,kc->scj", terms, column_pick, precision=HIGH)
        column_terms = lax.psum_scatter(
            partial_value.reshape(scenarios, across_link * tile_width),
            "link",
            scatter_dimension=1,
            tiled=True,
        )
        linked = linkage.astype(jnp.bfloat16)
        linked_block = lax.dynamic_slice_in_dim(linked, target * tile_width, tile_width, 1)
        gradient = column_terms - jnp.einsum(
            "si,ij->sj", linked_block, linkage_slab, preferred_element_type=jnp.float32
        )
        primal_new = jnp.maximum(primal - step_p * (column_cost[None, :] - gradient), 0.0)
        capacity_new = jnp.maximum(capacity - step_p * (cost_work[None, :] - linkage), 0.0)
        extrap = (2.0 * primal_new - primal).astype(jnp.bfloat16)
        capacity_bar = 2.0 * capacity_new - capacity
        forward_gathered = lax.all_gather(extrap, "link", axis=1, tiled=True).reshape(
            scenarios, across_link, tile_width
        )
        row_picked = jnp.take(forward_gathered, column_ids, axis=1)
        row_terms = jnp.einsum(
            "skj,kij->ski", row_picked, slabs, preferred_element_type=jnp.float32
        )
        forward_partial_value = jnp.einsum(
            "ski,kp->spi", row_terms, row_pick, precision=HIGH
        ).reshape(scenarios, across_tile * tile_width)
        link_term = jnp.einsum(
            "sj,ij->si", extrap, linkage_slab, preferred_element_type=jnp.float32
        )
        link_partial = (link_term[:, None, :] * link_pick[None, :, None]).reshape(
            scenarios, across_link * tile_width
        )
        row_result = lax.psum_scatter(
            forward_partial_value, "tile", scatter_dimension=1, tiled=True
        )
        link_result = lax.psum(link_partial, ("region", "tile", "link"))
        row_result, link_result = (row_result, link_result)
        duals_new = jnp.maximum(duals + step_d * (demand_work - row_result), 0.0)
        linkage_new = jnp.maximum(
            linkage + step_d * (bound_work[None, :] - (capacity_bar - link_result)), 0.0
        )
        primal, capacity, duals, linkage = (primal_new, capacity_new, duals_new, linkage_new)
        history.append([primal, capacity, duals, linkage])
    for entry in history:
        entry[1] = lax.dynamic_slice_in_dim(
            entry[1], lax.axis_index("link") * tile_width, tile_width, 1
        )
        entry[3] = lax.dynamic_slice_in_dim(
            entry[3], lax.axis_index("link") * tile_width, tile_width, 1
        )
    weight = (mean_count * (1 - restart)).astype(jnp.float32)[:, None]
    means = (primal_mean, capacity_mean, duals_mean, linkage_mean)
    averages = [
        (weight * means[i] + history[0][i] + history[1][i]) / (weight + 2.0) for i in range(4)
    ]
    counted = ((lax.axis_index("region") == 0) & (lax.axis_index("tile") == 0)).astype(jnp.float32)
    local_move = jnp.sum((history[1][0] - primal_start) ** 2, axis=1) + jnp.sum(
        (history[1][2] - duals_start) ** 2, axis=1
    )
    local_move = local_move + counted * (
        jnp.sum((history[1][1] - capacity_start) ** 2, axis=1)
        + jnp.sum((history[1][3] - linkage_start) ** 2, axis=1)
    )
    movement = lax.psum(local_move, ("region", "tile", "link"))
    return (
        history[1][0],
        history[1][1],
        history[1][2],
        history[1][3],
        averages[0],
        averages[1],
        averages[2],
        averages[3],
        movement,
    )


def solution(mesh):
    return jax.shard_map(
        on_device,
        mesh=mesh,
        in_specs=(
            P("region", "tile", "link", None, None),
            P("region", "tile", "link"),
            P("region", "tile", "link"),
            P("region", "tile", "link"),
            P("region", "tile", "link", None, None),
            P("region", "tile", "link"),
            P(("region", "tile", "link")),
            P("link"),
            P(None, ("region", "tile", "link")),
            P("link"),
            P(None, ("region", "tile", "link")),
            P(None, "link"),
            P(None, ("region", "tile", "link")),
            P(None, "link"),
            P(None, ("region", "tile", "link")),
            P(None, "link"),
            P(None, ("region", "tile", "link")),
            P(None, "link"),
            P(),
            P(),
            P(),
            P(),
        ),
        out_specs=(
            P(None, ("region", "tile", "link")),
            P(None, "link"),
            P(None, ("region", "tile", "link")),
            P(None, "link"),
            P(None, ("region", "tile", "link")),
            P(None, "link"),
            P(None, ("region", "tile", "link")),
            P(None, "link"),
            P(),
        ),
        check_vma=False,
    )
```

profile of v0, /device:TPU:1, one launch (start us, length us, event | category | flops | bytes accessed | tf_op | source)
XLA Modules:
  0.0 1319.6 jit_solution(7553416250620448696)
XLA Ops:
  10.0 1.0 fusion.70
  10.9 30.5 %all_gather.24 = bf16[32,4096]{1,0:T(8,128)(2,1)S(1)} all-gather(bf16[32,256]{1,0:T(8,128)(2,1)S(1)} %get-tuple-element.25), channel_id=1, replica_groups=mesh['region'=4,'tile'=16,'link'=8] {'tile'}, dimensions={1}, use_global_device_ids=true | all-gather | bytes 278528 | tf_op jit(solution)/shard_map/all_gather | solution.py:68
  44.3 21.2 %all_gather.25 = f32[32,2048]{1,0:T(8,128)S(1)} all-gather(f32[32,256]{1,0:T(8,128)S(1)} %get-tuple-element.36), channel_id=1, replica_groups=mesh['region'=4,'tile'=16,'link'=8] {'link'}, dimensions={1}, use_global_device_ids=true | all-gather | bytes 294912 | tf_op jit(solution)/shard_map/all_gather | solution.py:61
  65.5 18.0 %reduce-scatter.5.cloned.1.call-done = f32[32,256]{1,0:T(8,128)} async-done(((f32[32,2048]{1,0:T(8,128)}), f32[32,256]{1,0:T(8,128)}) %reduce-scatter.5.cloned.1.call-update) | async-done | bytes 32784 | tf_op jit(solution)/shard_map/reduce_scatter | solution.py:74
  83.4 0.9 subtract_convert_fusion.1
  84.4 14.9 %all_gather.26 = bf16[32,2048]{1,0:T(8,128)(2,1)S(1)} all-gather(bf16[32,256]{1,0:T(8,128)(2,1)S(1)} %get-tuple-element.38), channel_id=1, replica_groups=mesh['region'=4,'tile'=16,'link'=8] {'link'}, dimensions={1}, use_global_device_ids=true | all-gather | bytes 147456 | tf_op jit(solution)/shard_map/all_gather | solution.py:89
  100.8 1.1 copy.48
  103.8 55.5 %reduce-scatter.7.cloned.1.call-done = f32[32,256]{1,0:T(8,128)} async-done(((f32[32,4096]{1,0:T(8,128)}), f32[32,256]{1,0:T(8,128)}) %reduce-scatter.7.cloned.1.call-update) | async-done | bytes 32784 | tf_op jit(solution)/shard_map/reduce_scatter | solution.py:105
  159.4 0.8 fusion.69
  160.2 22.4 %all_gather.27 = bf16[32,4096]{1,0:T(8,128)(2,1)S(1)} all-gather(bf16[32,256]{1,0:T(8,128)(2,1)S(1)} %get-tuple-element.23), channel_id=1, replica_groups=mesh['region'=4,'tile'=16,'link'=8] {'tile'}, dimensions={1}, use_global_device_ids=true | all-gather | bytes 278528 | tf_op jit(solution)/shard_map/all_gather | solution.py:68
  183.9 0.8 copy.49
  184.7 31.4 %all_gather.29 = f32[32,2048]{1,0:T(8,128)S(1)} all-gather(f32[32,256]{1,0:T(8,128)S(1)} %get-tuple-element.35), channel_id=1, replica_groups=mesh['region'=4,'tile'=16,'link'=8] {'link'}, dimensions={1}, use_global_device_ids=true | all-gather | bytes 294912 | tf_op jit(solution)/shard_map/all_gather | solution.py:60
  216.8 10.2 all-gather.1
  227.7 8.1 all-gather
  235.8 393.9 %all-reduce.3.cloned.1.call-done = f32[32,2048]{1,0:T(8,128)} async-done(((f32[32,2048]{1,0:T(8,128)}), f32[32,2048]{1,0:T(8,128)}) %all-reduce.3.cloned.1.call-update) | async-done | bytes 262160 | tf_op jit(solution)/shard_map/psum | solution.py:108
  629.7 1.2 broadcast_multiply_fusion.2
  630.8 35.3 %reduce-scatter.9.cloned.1.call-done = f32[32,256]{1,0:T(8,128)} async-done(((f32[32,2048]{1,0:T(8,128)}), f32[32,256]{1,0:T(8,128)}) %reduce-scatter.9.cloned.1.call-update) | async-done | bytes 32784 | tf_op jit(solution)/shard_map/reduce_scatter | solution.py:74
  666.2 1.6 add_divide_fusion.3
  668.0 14.9 %all_gather.31 = bf16[32,2048]{1,0:T(8,128)(2,1)S(1)} all-gather(bf16[32,256]{1,0:T(8,128)(2,1)S(1)} %get-tuple-element.29), channel_id=1, replica_groups=mesh['region'=4,'tile'=16,'link'=8] {'link'}, dimensions={1}, use_global_device_ids=true | all-gather | bytes 147456 | tf_op jit(solution)/shard_map/all_gather | solution.py:89
  685.3 1.1 copy.52
  686.7 453.5 %all-reduce.5.cloned.1.call-done = f32[32,2048]{1,0:T(8,128)} async-done(((f32[32,2048]{1,0:T(8,128)}), f32[32,2048]{1,0:T(8,128)}) %all-reduce.5.cloned.1.call-update) | async-done | bytes 262160 | tf_op jit(solution)/shard_map/psum | solution.py:108
  1140.2 57.9 %reduce-scatter.11.cloned.1.call-done = f32[32,256]{1,0:T(8,128)} async-done(((f32[32,4096]{1,0:T(8,128)}), f32[32,256]{1,0:T(8,128)}) %reduce-scatter.11.cloned.1.call-update) | async-done | bytes 32784 | tf_op jit(solution)/shard_map/reduce_scatter | solution.py:105
  1198.1 1.6 multiply_reduce_fusion
  1199.7 112.4 %psum.23 = f32[32]{0:T(128)} all-reduce(f32[32]{0:T(128)S(1)} %multiply_add_fusion), channel_id=1, replica_groups=mesh['region'=4,'tile'=16,'link'=8] {'region','tile','link'}, use_global_device_ids=true, to_apply=%region_10.13 | all-reduce | flops 32 | bytes 256 | tf_op jit(solution)/shard_map/psum | solution.py:136
  (90 shorter events, 13.8 us)
Async XLA Ops:
  7.2 34.8 %copy-start = (bf16[1,1,8,256,256]{4,3,2,1,0:T(8,128)(2,1)S(1)}, bf16[1,1,8,256,256]{4,3,2,1,0:T(8,128)(2,1)}, u32[]{:S(2)}) copy-start(bf16[1,1,8,256,256]{4,3,2,1,0:T(8,128)(2,1)} %param.26) | copy-start | bytes 3145732
  7.2 76.2 %reduce-scatter.5.cloned.1.call-start = ((), (), s32[]{:S(2)}) async-start(), calls=%async_computation.4 | async-start | bytes 294912 | tf_op jit(solution)/shard_map/reduce_scatter | solution.py:74
  8.0 0.7 copy-start.17
  8.6 0.7 copy-start.12
  43.5 115.8 %reduce-scatter.7.cloned.1.call-start = ((), (), s32[]{:S(2)}) async-start(), calls=%async_computation.5 | async-start | bytes 557056 | tf_op jit(solution)/shard_map/reduce_scatter | solution.py:105
  44.3 39.2 %copy-start.1 = (bf16[1,1,1,256,256]{4,3,2,1,0:T(8,128)(2,1)S(1)}, bf16[1,1,1,256,256]{4,3,2,1,0:T(8,128)(2,1)}, u32[]{:S(2)}) copy-start(bf16[1,1,1,256,256]{4,3,2,1,0:T(8,128)(2,1)} %param.30) | copy-start | bytes 393220
  65.5 18.0 %copy-start.10 = (f32[32]{0:T(128)S(1)}, f32[32]{0:T(128)}, u32[]{:S(2)}) copy-start(f32[32]{0:T(128)} %param.46) | copy-start | bytes 388
  65.5 18.0 %copy-start.14 = (f32[256]{0:T(256)S(1)}, f32[256]{0:T(256)}, u32[]{:S(2)}) copy-start(f32[256]{0:T(256)} %param.32) | copy-start | bytes 3076
  101.9 527.7 %all-reduce.3.cloned.1.call-start = ((), (), s32[]{:S(2)}) async-start(), calls=%async_computation.7 | async-start | bytes 524288 | tf_op jit(solution)/shard_map/psum | solution.py:108
  102.0 0.7 copy-start.18
  103.7 55.6 %copy-start.4 = (f32[32,256]{1,0:T(8,128)S(1)}, f32[32,256]{1,0:T(8,128)}, u32[]{:S(2)}) copy-start(f32[32,256]{1,0:T(8,128)} %param.34) | copy-start | bytes 98308
  103.8 55.6 %copy-start.11 = (f32[32]{0:T(128)S(1)}, f32[32]{0:T(128)}, u32[]{:S(2)}) copy-start(f32[32]{0:T(128)} %param.47) | copy-start | bytes 388
  103.8 562.4 %reduce-scatter.9.cloned.1.call-start = ((), (), s32[]{:S(2)}) async-start(), calls=%async_computation.6 | async-start | bytes 294912 | tf_op jit(solution)/shard_map/reduce_scatter | solution.py:74
  184.7 955.5 %all-reduce.5.cloned.1.call-start = ((), (), s32[]{:S(2)}) async-start(), calls=%async_computation.9 | async-start | bytes 524288 | tf_op jit(solution)/shard_map/psum | solution.py:108
  216.2 0.7 copy-start.15
  227.0 0.7 copy-start.16
  629.7 36.5 %copy-start.7 = (f32[32,256]{1,0:T(8,128)S(1)}, f32[32,256]{1,0:T(8,128)}, u32[]{:S(2)}) copy-start(f32[32,256]{1,0:T(8,128)} %param.40) | copy-start | bytes 98308
  684.7 513.3 %reduce-scatter.11.cloned.1.call-start = ((), (), s32[]{:S(2)}) async-start(), calls=%async_computation.8 | async-start | bytes 557056 | tf_op jit(solution)/shard_map/reduce_scatter | solution.py:105
  686.5 511.5 %copy-start.2 = (f32[32,256]{1,0:T(8,128)S(1)}, f32[32,256]{1,0:T(8,128)}, u32[]{:S(2)}) copy-start(f32[32,256]{1,0:T(8,128)} %param.41) | copy-start | bytes 98308
  686.6 513.0 %copy-start.3 = (f32[32,256]{1,0:T(8,128)}, f32[32,256]{1,0:T(8,128)S(1)}, u32[]{:S(2)}) copy-start(f32[32,256]{1,0:T(8,128)S(1)} %get-tuple-element.16) | copy-start | bytes 98308
  1198.0 114.0 %copy-start.8 = (f32[32,256]{1,0:T(8,128)S(1)}, f32[32,256]{1,0:T(8,128)}, u32[]{:S(2)}) copy-start(f32[32,256]{1,0:T(8,128)} %param.42) | copy-start | bytes 98308
  1198.1 114.0 %copy-start.9 = (f32[32,256]{1,0:T(8,128)S(1)}, f32[32,256]{1,0:T(8,128)}, u32[]{:S(2)}) copy-start(f32[32,256]{1,0:T(8,128)} %param.43) | copy-start | bytes 98308
  1199.7 113.1 %copy-start.5 = (f32[32,256]{1,0:T(8,128)}, f32[32,256]{1,0:T(8,128)S(1)}, u32[]{:S(2)}) copy-start(f32[32,256]{1,0:T(8,128)S(1)} %get-tuple-element.14) | copy-start | bytes 98308
  1199.7 113.1 %copy-start.6 = (f32[32,256]{1,0:T(8,128)}, f32[32,256]{1,0:T(8,128)S(1)}, u32[]{:S(2)}) copy-start(f32[32,256]{1,0:T(8,128)S(1)} %get-tuple-element.34) | copy-start | bytes 98308
  (1 other events, 0.7 us)
Sparse Core Ops, SparseCore 0:
  43.7 39.7 reduce-scatter.4
  102.0 57.2 reduce-scatter.6
  164.8 464.8 all-reduce.2
  632.5 33.5 reduce-scatter.8
  684.8 455.2 all-reduce.4
  1143.0 54.9 reduce-scatter.10
where the time goes:
time: 1320 us
  waiting for transfers between devices  1010 us (77%)
  blocking collectives  266 us (20%)
  between operations  15.8 us (1%)
    psum x2, waiting for transfers between devices, on_device(): link_result = lax.psum(link_partial, ('region', 'tile', 'link'))  847 us
    reduce_scatter x2, waiting for transfers between devices, on_device(): lax.psum_scatter(forward_partial_value, 'tile', scatter_dimension=1, tile...  113 us
    psum x1, blocking collectives, on_device(): movement = lax.psum(local_move, ('region', 'tile', 'link'))  112 us
    reduce_scatter x2, waiting for transfers between devices, on_device(): lax.psum_scatter(partial_value.reshape(scenarios, across_link * tile_widt...  53.3 us
    all_gather x2, blocking collectives, on_device(): lax.all_gather(duals.astype(jnp.bfloat16), 'tile', axis=1, tiled=True)  52.9 us
    all_gather x1, blocking collectives, on_device(): lax.all_gather(capacity_start, 'link', axis=1, tiled=True)  31.4 us
    all_gather x2, blocking collectives, on_device(): lax.all_gather(extrap, 'link', axis=1, tiled=True)  29.8 us
  transfers between devices with their start and end apart: 6, of which 6 were waited for; matrix products, arithmetic and copies ran while one was open for 1% of the time, Pallas kernels for 0%

commit v1 on v0

v1 whole, which is shorter than its diff:
```python
import types

import jax
import jax.numpy as jnp
from jax import lax
from jax.experimental import pallas as pl
from jax.experimental.pallas import tpu as pltpu
from jax.sharding import PartitionSpec as P

REGION, TILE, LINK = SPLIT = ("region", "tile", "link")
MESH = pl.DeviceIdType.MESH
F32 = jnp.float32
BF16 = jnp.bfloat16
HALVES = 2
SWEEPS = 2
NEAR = (1, -1, 2, -2)
FAR = 5
N_SEMS = 280
VMEM_LIMIT = 62 * 1024 * 1024
Z_PARTNERS = (FAR, -FAR, 3, -3, 2, -2, 1, -1)


def dot_nn(a, b):
    return lax.dot_general(a, b, (((1,), (0,)), ((), ())), preferred_element_type=F32)


def dot_nt(a, b):
    return lax.dot_general(a, b, (((1,), (1,)), ((), ())), preferred_element_type=F32)


def kernel(n_region, n_tile, n_link, out, moved_out, refs):
    r, t, l = lax.axis_index(REGION), lax.axis_index(TILE), lax.axis_index(LINK)
    tile_row, tile_col, tile_count, linkage_block = refs.rows, refs.cols, refs.count, refs.target
    scen, width = refs.y.shape[1:]
    slots = refs.tiles_v.shape[0]
    half = scen // HALVES
    piece = scen // n_region
    ssem, rsem = refs.ssem, refs.rsem
    used = [0]
    sent = []

    def z_dev(offset):
        return (r, lax.rem(t + (offset + n_tile), n_tile), l)

    def link_dev(offset):
        return (r, t, lax.rem(l + offset, n_link))

    def region_dev(offset):
        return (lax.rem(r + offset, n_region), t, l)

    def send(src, dst, dev):
        i = used[0]
        used[0] = i + 1
        assert i < N_SEMS
        c = pltpu.make_async_remote_copy(
            src_ref=src, dst_ref=dst, send_sem=ssem.at[i], recv_sem=rsem.at[i], device_id=dev, device_id_type=MESH
        )
        c.start()
        sent.append(c)
        return c

    barrier = pltpu.get_barrier_semaphore()
    for o in Z_PARTNERS:
        pl.semaphore_signal(barrier, inc=1, device_id=z_dev(o), device_id_type=MESH)
    for o in range(1, n_link):
        pl.semaphore_signal(barrier, inc=1, device_id=link_dev(o), device_id_type=MESH)
    for o in range(1, n_region):
        pl.semaphore_signal(barrier, inc=1, device_id=region_dev(o), device_id_type=MESH)

    def load(i, src, dst):
        c = pltpu.make_async_copy(src, dst, refs.lsem.at[i])
        c.start()
        return c

    duals_loads = [load(0, refs.duals_now, refs.duals_now_v), load(1, refs.duals_mean, refs.duals_mean_v)]
    linkage_loads = [load(2, refs.linkage_now, refs.linkage_now_v), load(3, refs.linkage_mean, refs.linkage_mean_v)]
    other_loads = [
        load(4, refs.tiles, refs.tiles_v),
        load(5, refs.ltile, refs.ltile_v),
        load(6, refs.demand, refs.demand_v),
        load(7, refs.primal_now, refs.primal_now_v),
        load(8, refs.primal_mean, refs.primal_mean_v),
        load(9, refs.capacity_now, refs.capacity_now_v),
        load(10, refs.capacity_mean, refs.capacity_mean_v),
    ]

    eye = lax.broadcasted_iota(jnp.int32, (scen, scen), 0) == lax.broadcasted_iota(jnp.int32, (scen, scen), 1)

    def column(row):
        return jnp.sum(jnp.where(eye, jnp.broadcast_to(row, (scen, scen)), 0.0), axis=1, keepdims=True)

    restart_row = refs.restart[...].astype(F32)
    restarted = jnp.broadcast_to(column(restart_row), (scen, width)) == 1.0
    weight = jnp.broadcast_to(column(refs.mean_count[...].astype(F32) * (1.0 - restart_row)), (scen, width))
    step_p = jnp.broadcast_to(column(refs.primal_step[...]), (scen, width))
    step_d = jnp.broadcast_to(column(refs.dual_step[...]), (scen, width))

    def part(value, h):
        return value[h * half : (h + 1) * half]

    def rows_of(h):
        return pl.ds(h * half, half)

    live = tile_count[0, 0, 0]
    row_at, col_at = [], []
    for k in range(slots):
        dead = jnp.where(k < live, 0, -64)
        row_at.append(lax.rem(tile_row[0, 0, k] - t + n_tile, n_tile) + dead)
        col_at.append(lax.rem(tile_col[0, 0, k] - l + n_link, n_link) + dead)
    row_slot = [lax.rem(tile_row[0, 0, k] - t + n_tile, n_tile) for k in range(slots)]
    col_slot = [lax.rem(tile_col[0, 0, k] - l + n_link, n_link) for k in range(slots)]
    target_at = lax.rem(linkage_block[0, 0, 0] - l + n_link, n_link)

    x, y, z, w = refs.x, refs.y, refs.z, refs.w
    for c in duals_loads:
        c.wait()
    y[0] = jnp.where(restarted, refs.duals_mean_v[...], refs.duals_now_v[...])
    for h in range(HALVES):
        refs.yg[0][h][0] = y[0, rows_of(h), :].astype(BF16)
    for c in linkage_loads:
        c.wait()
    w[0] = jnp.where(restarted, refs.linkage_mean_v[...], refs.linkage_now_v[...])
    refs.wg[0][0] = w[0].astype(BF16)

    pl.semaphore_wait(barrier, len(Z_PARTNERS) + n_link - 1 + n_region - 1)

    def duals_send(s, h):
        g = refs.yg[s][h]
        out = {}
        for d in (FAR, -FAR) + NEAR:
            slot = -d % n_tile
            out[slot] = send(g.at[0], g.at[slot], z_dev(d))
        return out

    def duals_forward(s, h, out):
        g = refs.yg[s][h]
        order = (-3, -2, -1, 1, 2) if h == 0 else (-2, -1, 1, 2)
        back = (3, 2, 1, -1, -2) if h == 1 else (2, 1, -1, -2)
        for slot, moves in ((FAR, order), (n_tile - FAR, back)):
            out.pop(slot).wait_recv()
            for d in moves:
                to = (slot - d) % n_tile
                out[to] = send(g.at[slot], g.at[to], z_dev(d))

    def link_gather(buf):
        out = []
        for d in range(1, n_link):
            out.append(send(buf.at[0], buf.at[-d % n_link], link_dev(d)))
        return out

    def finish(copies):
        for c in copies:
            c.wait_recv()

    def picked(at, terms, offset):
        total = None
        for k in range(slots):
            one = jnp.where(at[k] == offset, 1.0, 0.0) * terms[k]
            total = one if total is None else total + one
        return total

    def columns_send(s, h):
        g = refs.yg[s][h]
        terms = [dot_nn(g[row_slot[k]], refs.tiles_v[k]) for k in range(slots)]
        out = refs.cout[s][h]
        copies = []
        for o in list(range(1, n_link)) + [0]:
            out[o] = picked(col_at, terms, o)
            if o:
                copies.append(send(out.at[o], refs.cin[s][h].at[o], link_dev(o)))
        return copies

    def primal_update(s, h):
        total = refs.cout[s][h][0]
        for o in range(1, n_link):
            total = total + refs.cin[s][h][o]
        linked = refs.wg[s][target_at]
        gradient = total - dot_nn(part(linked, h), refs.ltile_v[...])
        old = x[s, rows_of(h), :]
        new = jnp.maximum(old - part(step_p, h) * (refs.column_cost[...] - gradient), 0.0)
        x[s + 1, rows_of(h), :] = new
        extrap = (2.0 * new - old).astype(BF16)
        refs.eg[s][h][0] = extrap

    def rows_send(s, h):
        g = refs.eg[s][h]
        terms = [dot_nt(g[col_slot[k]], refs.tiles_v[k]) for k in range(slots)]
        out, near = refs.rout[s][h], refs.rnear[s][h]
        third = 3 if h == 0 else -3
        relay, direct = [], []
        for i, e in enumerate(NEAR):
            out[i, 0] = picked(row_at, terms, (-e - FAR) % n_tile)
            out[i, 1] = picked(row_at, terms, (-e + FAR) % n_tile)
            relay.append(send(out.at[i], refs.rin[s][h].at[i], z_dev(-e)))
            if i == 0:
                out[4, 0] = picked(row_at, terms, n_tile // 2)
                relay.append(send(out.at[4, 0], refs.rin[s][h].at[4, 0], z_dev(-third)))
        for i, e in enumerate(NEAR):
            near[i] = picked(row_at, terms, -e % n_tile)
        near[4] = picked(row_at, terms, n_tile - FAR)
        near[5] = picked(row_at, terms, FAR)
        near[6] = picked(row_at, terms, 0)
        return relay, direct

    def rows_direct(s, h, direct):
        for i, e in enumerate(NEAR):
            direct.append(send(refs.rnear[s][h].at[i], refs.rdir[s][h].at[i], z_dev(-e)))

    def rows_relay(s, h, relay, direct):
        finish(relay)
        got, near = refs.rin[s][h], refs.rnear[s][h]
        for j in range(2):
            total = near[4 + j]
            for i in range(4):
                total = total + got[i, j]
            if j == h:
                total = total + got[4, 0]
            near[4 + j] = total
            direct.append(send(near.at[4 + j], refs.rdir[s][h].at[4 + j], z_dev(FAR if j else -FAR)))

    def duals_update(s, h, direct):
        finish(direct)
        total = refs.rnear[s][h][6]
        for i in range(6):
            total = total + refs.rdir[s][h][i]
        rows = rows_of(h)
        new = jnp.maximum(y[s, rows, :] + part(step_d, h) * (refs.demand_v[rows, :] - total), 0.0)
        y[s + 1, rows, :] = new
        if s + 1 < SWEEPS:
            refs.yg[s + 1][h][0] = new.astype(BF16)

    def linking_start(s):
        out = refs.lout[s]
        e = jnp.concatenate([refs.eg[s][h][0] for h in range(HALVES)], axis=0)
        term = dot_nt(e, refs.ltile_v[...])
        copies = []
        for o in list(range(1, n_link)) + [0]:
            out[o] = jnp.where(target_at == o, 1.0, 0.0) * term
            if o:
                copies.append(send(out.at[o], refs.lin[s].at[o], link_dev(o)))
        return copies

    def linking_region(s, copies):
        finish(copies)
        total = refs.lout[s][0]
        for o in range(1, n_link):
            total = total + refs.lin[s][o]
        own = refs.lsum[s]
        own[...] = total
        got = refs.lreg[s]
        result = []
        for o in range(1, n_region):
            to = lax.rem(r + o, n_region)
            rows = pl.ds(pl.multiple_of(to * piece, piece), piece)
            result.append(send(own.at[rows, :], got.at[r], region_dev(o)))
        got[r] = own[pl.ds(pl.multiple_of(r * piece, piece), piece), :]
        return result

    def summed(ref, n):
        total = ref[0]
        for i in range(1, n):
            total = total + ref[i]
        return total

    def spread(buf, at, value, devs):
        buf[at] = value
        return [send(buf.at[at], buf.at[at], d) for d in devs]

    region_devs = [region_dev(o) for o in range(1, n_region)]
    link_devs = [link_dev(o) for o in range(1, n_link)]

    def z_spread(buf, value):
        buf[t] = value
        return {d: send(buf.at[t], buf.at[t], z_dev(-d)) for d in (FAR, -FAR) + NEAR}

    def z_relay(buf, out):
        for d, moves in ((FAR, (-3, -2, -1, 1, 2)), (-FAR, (2, 1, -1, -2))):
            out.pop(d).wait_recv()
            at = lax.rem(t + (d + n_tile), n_tile)
            for m in moves:
                out[d, m] = send(buf.at[at], buf.at[at], z_dev(m))

    def linking_z(s, copies):
        finish(copies)
        return z_spread(refs.lz[s], summed(refs.lreg[s], n_region))

    def linking_back(s, copies):
        finish(copies.values())
        return spread(refs.lback[s], r, summed(refs.lz[s], n_tile), region_devs)

    def capacity_update(s):
        z[s + 1] = jnp.maximum(z[s] - step_p * (refs.capacity_cost[...] - w[s]), 0.0)

    def linking_update(s, copies):
        finish(copies)
        back = refs.lback[s]
        total = jnp.concatenate([back[i] for i in range(n_region)], axis=0)
        bar = 2.0 * z[s + 1] - z[s]
        w[s + 1] = jnp.maximum(w[s] + step_d * (refs.linkage_bound[...] - (bar - total)), 0.0)

    def average(mean, state, i):
        out[i] = (weight * mean + state[1] + state[2]) / (weight + 2.0)

    ready = [duals_send(0, h) for h in range(HALVES)]
    w_copies = link_gather(refs.wg[0])
    for c in other_loads:
        c.wait()
    x[0] = jnp.where(restarted, refs.primal_mean_v[...], refs.primal_now_v[...])
    z[0] = jnp.where(restarted, refs.capacity_mean_v[...], refs.capacity_now_v[...])

    link_copies = None
    for s in range(SWEEPS):
        last = s + 1 == SWEEPS
        for h in range(HALVES):
            duals_forward(s, h, ready[h])
        if s:
            link_copies = linking_back(s - 1, link_copies)
        columns = []
        for h in range(HALVES):
            finish(ready[h].values())
            columns.append(columns_send(s, h))
        if s:
            linking_update(s - 1, link_copies)
            refs.wg[s][0] = w[s].astype(BF16)
            w_copies = link_gather(refs.wg[s])
        capacity_update(s)
        finish(w_copies)
        gathers = []
        for h in range(HALVES):
            finish(columns[h])
            primal_update(s, h)
            gathers.append(link_gather(refs.eg[s][h]))
        link_copies = linking_start(s)
        relays = []
        for h in range(HALVES):
            finish(gathers[h])
            relays.append(rows_send(s, h))
        for h in range(HALVES):
            rows_direct(s, h, relays[h][1])
        link_copies = linking_region(s, link_copies)
        for h in range(HALVES):
            rows_relay(s, h, *relays[h])
        link_copies = linking_z(s, link_copies)
        if last:
            out[0] = x[2]
            out[1] = z[2]
            average(refs.primal_mean_v[...], x, 4)
            average(refs.capacity_mean_v[...], z, 5)
        for h in range(HALVES):
            duals_update(s, h, relays[h][1])
            if not last:
                ready[h] = duals_send(s + 1, h)
        z_relay(refs.lz[s], link_copies)

    def squares(state):
        return jnp.sum((state[2] - state[0]) ** 2, axis=1, keepdims=True)

    def as_row(col):
        lanes = refs.mz.shape[-1]
        on = lax.broadcasted_iota(jnp.int32, (scen, lanes), 0) == lax.broadcasted_iota(jnp.int32, (scen, lanes), 1)
        return jnp.sum(jnp.where(on, jnp.broadcast_to(col, (scen, lanes)), 0.0), axis=0, keepdims=True)

    copies = z_spread(refs.mz, as_row(squares(x) + squares(y)))
    out[2] = y[2]
    average(refs.duals_mean_v[...], y, 6)
    z_relay(refs.mz, copies)
    link_copies = linking_back(SWEEPS - 1, link_copies)
    finish(copies.values())
    copies = spread(refs.mreg, r, summed(refs.mz, n_tile), region_devs)
    linking_update(SWEEPS - 1, link_copies)
    moved = as_row(squares(z) + squares(w))
    out[3] = w[2]
    average(refs.linkage_mean_v[...], w, 7)
    finish(copies)
    copies = spread(refs.mlink, l, summed(refs.mreg, n_region) + moved, link_devs)
    finish(copies)
    moved_out[...] = summed(refs.mlink, n_link)
    for c in sent:
        c.wait_send()


def on_device(
    tiles, tile_row, tile_col, tile_count, linkage_tiles, linkage_block, column_cost, capacity_cost, demand,
    linkage_bound, primal_now, capacity_now, duals_now, linkage_now, primal_mean, capacity_mean, duals_mean,
    linkage_mean, restart, mean_count, primal_step, dual_step,
):
    n_region, n_tile, n_link = (lax.axis_size(a) for a in SPLIT)
    scen, width = primal_now.shape
    slots = tile_row.shape[2]
    half = scen // HALVES
    piece = scen // n_region
    smem = pl.BlockSpec(memory_space=pltpu.SMEM)
    vmem = pl.BlockSpec(memory_space=pltpu.VMEM)
    hbm = pl.BlockSpec(memory_space=pltpu.HBM)
    anywhere = pl.BlockSpec(memory_space=pl.ANY)
    inputs = dict(
        rows=(tile_row, smem),
        cols=(tile_col, smem),
        count=(tile_count, smem),
        target=(linkage_block, smem),
        restart=(restart.reshape(1, scen), vmem),
        mean_count=(mean_count.reshape(1, scen), vmem),
        primal_step=(primal_step.reshape(1, scen), vmem),
        dual_step=(dual_step.reshape(1, scen), vmem),
        column_cost=(column_cost.reshape(1, width), vmem),
        capacity_cost=(capacity_cost.reshape(1, width), vmem),
        linkage_bound=(linkage_bound.reshape(1, width), vmem),
        tiles=(tiles.reshape(slots, width, width), hbm),
        ltile=(linkage_tiles.reshape(width, width), hbm),
        demand=(demand, hbm),
        primal_now=(primal_now, hbm),
        capacity_now=(capacity_now, hbm),
        duals_now=(duals_now, hbm),
        linkage_now=(linkage_now, hbm),
        primal_mean=(primal_mean, hbm),
        capacity_mean=(capacity_mean, hbm),
        duals_mean=(duals_mean, hbm),
        linkage_mean=(linkage_mean, hbm),
    )
    results = jax.ShapeDtypeStruct((8, scen, width), F32)
    moved = jax.ShapeDtypeStruct((1, 128), F32)
    block = pltpu.VMEM((scen, width), F32)

    def per_sweep(shape, dtype):
        return [pltpu.VMEM(shape, dtype)] * SWEEPS

    def per_half(shape, dtype):
        return [[pltpu.VMEM(shape, dtype)] * HALVES] * SWEEPS

    scratch = dict(
        ssem=pltpu.SemaphoreType.DMA((N_SEMS,)),
        rsem=pltpu.SemaphoreType.DMA((N_SEMS,)),
        lsem=pltpu.SemaphoreType.DMA((11,)),
        tiles_v=pltpu.VMEM((slots, width, width), BF16),
        ltile_v=pltpu.VMEM((width, width), BF16),
        mz=pltpu.VMEM((n_tile, 1, 128), F32),
        mreg=pltpu.VMEM((n_region, 1, 128), F32),
        mlink=pltpu.VMEM((n_link, 1, 128), F32),
        duals_now_v=block,
        duals_mean_v=block,
        linkage_now_v=block,
        linkage_mean_v=block,
        primal_now_v=block,
        primal_mean_v=block,
        capacity_now_v=block,
        capacity_mean_v=block,
        demand_v=block,
        x=pltpu.VMEM((SWEEPS + 1, scen, width), F32),
        y=pltpu.VMEM((SWEEPS + 1, scen, width), F32),
        z=pltpu.VMEM((SWEEPS + 1, scen, width), F32),
        w=pltpu.VMEM((SWEEPS + 1, scen, width), F32),
        wg=per_sweep((n_link, scen, width), BF16),
        lout=per_sweep((n_link, scen, width), F32),
        lin=per_sweep((n_link, scen, width), F32),
        lsum=per_sweep((scen, width), F32),
        lreg=per_sweep((n_region, piece, width), F32),
        lz=per_sweep((n_tile, piece, width), F32),
        lback=per_sweep((n_region, piece, width), F32),
        yg=per_half((n_tile, half, width), BF16),
        eg=per_half((n_link, half, width), BF16),
        cout=per_half((n_link, half, width), F32),
        cin=per_half((n_link, half, width), F32),
        rout=per_half((5, 2, half, width), F32),
        rin=per_half((5, 2, half, width), F32),
        rnear=per_half((7, half, width), F32),
        rdir=per_half((6, half, width), F32),
    )

    def body(ins, out, moved_out, scr):
        kernel(n_region, n_tile, n_link, out, moved_out, types.SimpleNamespace(**ins, **scr))

    packed, moved = pl.pallas_call(
        body,
        out_shape=(results, moved),
        in_specs=({k: v[1] for k, v in inputs.items()},),
        out_specs=(vmem, vmem),
        scratch_shapes=(scratch,),
        compiler_params=pltpu.CompilerParams(
            collective_id=0, has_side_effects=True, vmem_limit_bytes=VMEM_LIMIT
        ),
        cost_estimate=pl.CostEstimate(flops=80_000_000, bytes_accessed=2_000_000, transcendentals=0),
        name="pdhg",
    )({k: v[0] for k, v in inputs.items()})

    def split(src, row, *rest):
        outs, moved_cut, sem = rest[:8], rest[8], rest[9]
        copies = [pltpu.make_async_copy(src.at[i], outs[i], sem.at[i]) for i in range(8)]
        for c in copies:
            c.start()
        moved_cut[...] = row[:, :scen]
        for c in copies:
            c.wait()

    one = jax.ShapeDtypeStruct((scen, width), F32)
    *outs, cut = pl.pallas_call(
        split,
        out_shape=[one] * 8 + [jax.ShapeDtypeStruct((1, scen), F32)],
        in_specs=[vmem, vmem],
        out_specs=[anywhere] * 8 + [vmem],
        scratch_shapes=[pltpu.SemaphoreType.DMA((8,))],
        name="split",
    )(packed, moved)
    return (*outs, cut.reshape(scen))


def solution(mesh):
    blocked = P(None, SPLIT)
    shared = P(None, LINK)
    tiled = P(REGION, TILE, LINK)
    slabs = P(REGION, TILE, LINK, None, None)
    states = (blocked, shared, blocked, shared)
    return jax.shard_map(
        on_device,
        mesh=mesh,
        in_specs=(
            slabs, tiled, tiled, tiled, slabs, tiled, P(SPLIT), P(LINK), blocked, P(LINK),
            *states, *states, P(), P(), P(), P(),
        ),
        out_specs=(*states, *states, P()),
        check_vma=False,
    )
```

time: 1320 us -> 115 us (0.09)
  waiting for transfers between devices: 1010 us -> 0 us
  blocking collectives: 266 us -> 0 us
  Pallas kernels: 0 us -> 113 us
  between operations: 15.8 us -> 1.95 us
    psum x2 -> x0, waiting for transfers between devices: 847 us -> none  [on_device(): link_result = lax.psum(link_partial, ('region', 'tile', 'link'))]
    reduce_scatter x4 -> x0, waiting for transfers between devices: 167 us -> none  [the longest x2 113 us: on_device(): lax.psum_scatter(forward_partial_value, 'tile', scatter_dimension=1, tile...]
    all_gather x8 -> x0, blocking collectives: 153 us -> none  [the longest x2 52.9 us: on_device(): lax.all_gather(duals.astype(jnp.bfloat16), 'tile', axis=1, tiled=True)]
    pallas_call x0 -> x2, Pallas kernels: none -> 113 us  [the longest x1 110 us: on_device(): pl.pallas_call(body, out_shape=(results, moved), in_specs=({k: v[1] for k...]
    psum x1 -> x0, blocking collectives: 112 us -> none  [on_device(): movement = lax.psum(local_move, ('region', 'tile', 'link'))]
  transfers between devices with their start and end apart: 6 -> 0, of which waited for: 6 -> 0; matrix products, arithmetic and copies ran while one was open for 1% -> 0% of each run, Pallas kernels for 0% -> 0%
where the time goes in v1:
time: 115 us
  Pallas kernels  113 us (98%)
  between operations  1.95 us (2%)
    pallas_call x1, Pallas kernels, on_device(): pl.pallas_call(body, out_shape=(results, moved), in_specs=({k: v[1] for k...  110 us

profile of v1, /device:TPU:1, one launch (start us, length us, event | category | flops | bytes accessed | tf_op | source)
XLA Modules:
  0.0 114.6 jit_solution(15469890937902423861)
XLA Ops:
  1.9 110.4 %pdhg.1 = (f32[8,32,256]{2,1,0:T(8,128)}, f32[1,128]{1,0:T(1,128)}) custom-call(f32[1,256]{1,0:T(1,128)} %bitcast.12, f32[32,256]{1,0:T(8,128)} %ins__capacity_mean__.1, f32[32,256]{1,0:T(8,128)} %ins__capacity_now__.1, s32[1,1,8]{2,1,0:T(1,128)} %ins__cols__.1, f32[1,256]{1,0:T(1,128)} %bitcast.13, s32[1,1,1]{2,1,0:T(1,128)S(6)} %copy.31.ins__count__, ...), custom_call_target="tpu_custom_call" | custom-call | flops 80000000 | bytes 2000000 | tf_op jit(solution)/shard_map/pdhg/pallas_call | solution.py:472
  112.4 2.2 %split.1 = (f32[32,256]{1,0:T(8,128)}, f32[32,256]{1,0:T(8,128)}, f32[32,256]{1,0:T(8,128)}, f32[32,256]{1,0:T(8,128)}, f32[32,256]{1,0:T(8,128)}, /*index=5*/f3...) custom-call(f32[8,32,256]{2,1,0:T(8,128)} %get-tuple-element.20.src, ...), custom_call_target="tpu_custom_call" | custom-call | tf_op jit(solution)/shard_map/split/pallas_call | solution.py:495

commit v2 on v1

--- a/solution.py
+++ b/solution.py
@@ -15,7 +15,10 @@
 SWEEPS = 2
 NEAR = (1, -1, 2, -2)
 FAR = 5
-N_SEMS = 280
+N_SEMS = 360
+LANES = 128
+TOP = 32766.0
+I16 = jnp.int16
 VMEM_LIMIT = 62 * 1024 * 1024
 Z_PARTNERS = (FAR, -FAR, 3, -3, 2, -2, 1, -1)
 
@@ -159,21 +162,44 @@
             total = one if total is None else total + one
         return total
 
+    def lane_top(value, top):
+        value = jnp.abs(value)
+        for i in range(0, width, LANES):
+            top = jnp.maximum(top, jnp.max(value[:, i : i + LANES], axis=0, keepdims=True))
+        return top
+
+    def wide(row):
+        return jnp.concatenate([row] * (width // LANES), axis=1)
+
+    def fixed(value, inverse):
+        return jnp.round(value * inverse).astype(jnp.int32).astype(I16)
+
+    def loose(value, scale):
+        return value.astype(jnp.int32).astype(F32) * wide(scale)
+
+    least = jnp.full((1, LANES), 1e-30, F32)
+
     def columns_send(s, h):
         g = refs.yg[s][h]
         terms = [dot_nn(g[row_slot[k]], refs.tiles_v[k]) for k in range(slots)]
-        out = refs.cout[s][h]
+        parts, out, scale = refs.cpart[s][h], refs.cout[s][h], refs.cscale_out[s][h]
+        top = least
+        for o in range(n_link):
+            parts[o] = picked(col_at, terms, o)
+            top = lane_top(parts[o], top)
+        scale[...] = top * (1.0 / TOP)
+        inverse = wide(TOP / top)
         copies = []
-        for o in list(range(1, n_link)) + [0]:
-            out[o] = picked(col_at, terms, o)
-            if o:
-                copies.append(send(out.at[o], refs.cin[s][h].at[o], link_dev(o)))
+        for o in range(1, n_link):
+            copies.append(send(scale, refs.cscale[s][h].at[o], link_dev(o)))
+            out[o] = fixed(parts[o], inverse)
+            copies.append(send(out.at[o], refs.cin[s][h].at[o], link_dev(o)))
         return copies
 
     def primal_update(s, h):
-        total = refs.cout[s][h][0]
+        total = refs.cpart[s][h][0]
         for o in range(1, n_link):
-            total = total + refs.cin[s][h][o]
+            total = total + loose(refs.cin[s][h][o], refs.cscale[s][h][o])
         linked = refs.wg[s][target_at]
         gradient = total - dot_nn(part(linked, h), refs.ltile_v[...])
         old = x[s, rows_of(h), :]
@@ -185,44 +211,62 @@
     def rows_send(s, h):
         g = refs.eg[s][h]
         terms = [dot_nt(g[col_slot[k]], refs.tiles_v[k]) for k in range(slots)]
-        out, near = refs.rout[s][h], refs.rnear[s][h]
+        parts, out, near, scale = refs.rpart[s][h], refs.rout[s][h], refs.rnear[s][h], refs.rscale_out[s][h]
+        top = least
+        for o in range(n_tile):
+            parts[o] = picked(row_at, terms, o)
+            top = lane_top(parts[o], top)
+        scale[...] = top * (1.0 / TOP)
+        inverse = wide(TOP / top)
         third = 3 if h == 0 else -3
-        relay, direct = [], []
+        copies = []
         for i, e in enumerate(NEAR):
-            out[i, 0] = picked(row_at, terms, (-e - FAR) % n_tile)
-            out[i, 1] = picked(row_at, terms, (-e + FAR) % n_tile)
-            relay.append(send(out.at[i], refs.rin[s][h].at[i], z_dev(-e)))
+            copies.append(send(scale, refs.rscale[s][h].at[i], z_dev(-e)))
+            out[i, 0] = fixed(parts[(-e - FAR) % n_tile], inverse)
+            out[i, 1] = fixed(parts[(-e + FAR) % n_tile], inverse)
+            copies.append(send(out.at[i], refs.rin[s][h].at[i], z_dev(-e)))
             if i == 0:
-                out[4, 0] = picked(row_at, terms, n_tile // 2)
-                relay.append(send(out.at[4, 0], refs.rin[s][h].at[4, 0], z_dev(-third)))
+                copies.append(send(scale, refs.rscale[s][h].at[4], z_dev(-third)))
+                out[4, 0] = fixed(parts[n_tile // 2], inverse)
+                copies.append(send(out.at[4, 0], refs.rin[s][h].at[4, 0], z_dev(-third)))
         for i, e in enumerate(NEAR):
-            near[i] = picked(row_at, terms, -e % n_tile)
-        near[4] = picked(row_at, terms, n_tile - FAR)
-        near[5] = picked(row_at, terms, FAR)
-        near[6] = picked(row_at, terms, 0)
-        return relay, direct
-
-    def rows_direct(s, h, direct):
-        for i, e in enumerate(NEAR):
-            direct.append(send(refs.rnear[s][h].at[i], refs.rdir[s][h].at[i], z_dev(-e)))
-
-    def rows_relay(s, h, relay, direct):
-        finish(relay)
-        got, near = refs.rin[s][h], refs.rnear[s][h]
+            near[i] = fixed(parts[-e % n_tile], inverse)
+        return copies
+
+    def rows_direct(s, h):
+        return [
+            send(refs.rnear[s][h].at[i], refs.rdir[s][h].at[i], z_dev(-e)) for i, e in enumerate(NEAR)
+        ]
+
+    def rows_relay(s, h, copies):
+        finish(copies)
+        got, parts, scale = refs.rin[s][h], refs.rpart[s][h], refs.rscale[s][h]
+        totals, top = [], least
         for j in range(2):
-            total = near[4 + j]
+            total = parts[FAR if j else n_tile - FAR]
             for i in range(4):
-                total = total + got[i, j]
+                total = total + loose(got[i, j], scale[i])
             if j == h:
-                total = total + got[4, 0]
-            near[4 + j] = total
-            direct.append(send(near.at[4 + j], refs.rdir[s][h].at[4 + j], z_dev(FAR if j else -FAR)))
-
-    def duals_update(s, h, direct):
-        finish(direct)
-        total = refs.rnear[s][h][6]
-        for i in range(6):
-            total = total + refs.rdir[s][h][i]
+                total = total + loose(got[4, 0], scale[4])
+            totals.append(total)
+            top = lane_top(total, top)
+        refs.fscale_out[s][h][...] = top * (1.0 / TOP)
+        inverse = wide(TOP / top)
+        result = []
+        for j in range(2):
+            to = z_dev(FAR if j else -FAR)
+            result.append(send(refs.fscale_out[s][h], refs.fscale[s][h].at[j], to))
+            refs.rfar[s][h][j] = fixed(totals[j], inverse)
+            result.append(send(refs.rfar[s][h].at[j], refs.rfin[s][h].at[j], to))
+        return result
+
+    def duals_update(s, h, copies):
+        finish(copies)
+        total = refs.rpart[s][h][0]
+        for i in range(4):
+            total = total + loose(refs.rdir[s][h][i], refs.rscale[s][h][i])
+        for j in range(2):
+            total = total + loose(refs.rfin[s][h][j], refs.fscale[s][h][j])
         rows = rows_of(h)
         new = jnp.maximum(y[s, rows, :] + part(step_d, h) * (refs.demand_v[rows, :] - total), 0.0)
         y[s + 1, rows, :] = new
@@ -233,18 +277,22 @@
         out = refs.lout[s]
         e = jnp.concatenate([refs.eg[s][h][0] for h in range(HALVES)], axis=0)
         term = dot_nt(e, refs.ltile_v[...])
+        top = lane_top(term, least)
+        refs.lscale_out[s][...] = top * (1.0 / TOP)
+        scaled = term * wide(TOP / top)
+        refs.lsum[s][...] = jnp.where(target_at == 0, 1.0, 0.0) * term
         copies = []
-        for o in list(range(1, n_link)) + [0]:
-            out[o] = jnp.where(target_at == o, 1.0, 0.0) * term
-            if o:
-                copies.append(send(out.at[o], refs.lin[s].at[o], link_dev(o)))
+        for o in range(1, n_link):
+            copies.append(send(refs.lscale_out[s], refs.lscale[s].at[o], link_dev(o)))
+            out[o] = fixed(scaled, jnp.where(target_at == o, 1.0, 0.0))
+            copies.append(send(out.at[o], refs.lin[s].at[o], link_dev(o)))
         return copies
 
     def linking_region(s, copies):
         finish(copies)
-        total = refs.lout[s][0]
+        total = refs.lsum[s][...]
         for o in range(1, n_link):
-            total = total + refs.lin[s][o]
+            total = total + loose(refs.lin[s][o], refs.lscale[s][o])
         own = refs.lsum[s]
         own[...] = total
         got = refs.lreg[s]
@@ -331,15 +379,15 @@
             primal_update(s, h)
             gathers.append(link_gather(refs.eg[s][h]))
         link_copies = linking_start(s)
-        relays = []
+        relays, directs = [], []
         for h in range(HALVES):
             finish(gathers[h])
             relays.append(rows_send(s, h))
         for h in range(HALVES):
-            rows_direct(s, h, relays[h][1])
+            directs.append(rows_direct(s, h))
         link_copies = linking_region(s, link_copies)
         for h in range(HALVES):
-            rows_relay(s, h, *relays[h])
+            directs[h] += rows_relay(s, h, relays[h])
         link_copies = linking_z(s, link_copies)
         if last:
             out[0] = x[2]
@@ -347,10 +395,11 @@
             average(refs.primal_mean_v[...], x, 4)
             average(refs.capacity_mean_v[...], z, 5)
         for h in range(HALVES):
-            duals_update(s, h, relays[h][1])
+            duals_update(s, h, directs[h])
             if not last:
                 ready[h] = duals_send(s + 1, h)
-        z_relay(refs.lz[s], link_copies)
+        if not last:
+            z_relay(refs.lz[s], link_copies)
 
     def squares(state):
         return jnp.sum((state[2] - state[0]) ** 2, axis=1, keepdims=True)
@@ -363,6 +412,7 @@
     copies = z_spread(refs.mz, as_row(squares(x) + squares(y)))
     out[2] = y[2]
     average(refs.duals_mean_v[...], y, 6)
+    z_relay(refs.lz[SWEEPS - 1], link_copies)
     z_relay(refs.mz, copies)
     link_copies = linking_back(SWEEPS - 1, link_copies)
     finish(copies.values())
@@ -450,20 +500,32 @@
         z=pltpu.VMEM((SWEEPS + 1, scen, width), F32),
         w=pltpu.VMEM((SWEEPS + 1, scen, width), F32),
         wg=per_sweep((n_link, scen, width), BF16),
-        lout=per_sweep((n_link, scen, width), F32),
-        lin=per_sweep((n_link, scen, width), F32),
+        lout=per_sweep((n_link, scen, width), I16),
+        lin=per_sweep((n_link, scen, width), I16),
+        lscale=per_sweep((n_link, 1, LANES), F32),
+        lscale_out=per_sweep((1, LANES), F32),
         lsum=per_sweep((scen, width), F32),
         lreg=per_sweep((n_region, piece, width), F32),
         lz=per_sweep((n_tile, piece, width), F32),
         lback=per_sweep((n_region, piece, width), F32),
         yg=per_half((n_tile, half, width), BF16),
         eg=per_half((n_link, half, width), BF16),
-        cout=per_half((n_link, half, width), F32),
-        cin=per_half((n_link, half, width), F32),
-        rout=per_half((5, 2, half, width), F32),
-        rin=per_half((5, 2, half, width), F32),
-        rnear=per_half((7, half, width), F32),
-        rdir=per_half((6, half, width), F32),
+        cpart=per_half((n_link, half, width), F32),
+        cout=per_half((n_link, half, width), I16),
+        cin=per_half((n_link, half, width), I16),
+        cscale=per_half((n_link, 1, LANES), F32),
+        cscale_out=per_half((1, LANES), F32),
+        rpart=per_half((n_tile, half, width), F32),
+        rout=per_half((5, 2, half, width), I16),
+        rin=per_half((5, 2, half, width), I16),
+        rscale=per_half((5, 1, LANES), F32),
+        rscale_out=per_half((1, LANES), F32),
+        rnear=per_half((4, half, width), I16),
+        rdir=per_half((4, half, width), I16),
+        rfar=per_half((2, half, width), I16),
+        rfin=per_half((2, half, width), I16),
+        fscale=per_half((2, 1, LANES), F32),
+        fscale_out=per_half((1, LANES), F32),
     )
 
     def body(ins, out, moved_out, scr):

time: 115 us -> 106 us (0.922)
  Pallas kernels: 113 us -> 104 us
    pallas_call x1, Pallas kernels: 110 us -> 102 us  [on_device(): pl.pallas_call(body, out_shape=(results, moved), in_specs=({k: v[1] for k...]
where the time goes in v2:
time: 106 us
  Pallas kernels  104 us (98%)
  between operations  1.95 us (2%)
    pallas_call x1, Pallas kernels, on_device(): pl.pallas_call(body, out_shape=(results, moved), in_specs=({k: v[1] for k...  102 us
    pallas_call x1, Pallas kernels, on_device(): pl.pallas_call(split, out_shape=[one] * 8 + [jax.ShapeDtypeStruct((1, sce...  2.22 us

profile of v2, /device:TPU:1, one launch (start us, length us, event | category | flops | bytes accessed | tf_op | source)
XLA Modules:
  0.0 105.7 jit_solution(10778826961320869491)
XLA Ops:
  1.9 101.5 %pdhg.1 = (f32[8,32,256]{2,1,0:T(8,128)}, f32[1,128]{1,0:T(1,128)}) custom-call(f32[1,256]{1,0:T(1,128)} %bitcast.12, f32[32,256]{1,0:T(8,128)} %ins__capacity_mean__.1, f32[32,256]{1,0:T(8,128)} %ins__capacity_now__.1, s32[1,1,8]{2,1,0:T(1,128)} %ins__cols__.1, f32[1,256]{1,0:T(1,128)} %bitcast.13, s32[1,1,1]{2,1,0:T(1,128)S(6)} %copy.31.ins__count__, ...), custom_call_target="tpu_custom_call" | custom-call | flops 80000000 | bytes 2000000 | tf_op jit(solution)/shard_map/pdhg/pallas_call | solution.py:534
  103.5 2.2 %split.1 = (f32[32,256]{1,0:T(8,128)}, f32[32,256]{1,0:T(8,128)}, f32[32,256]{1,0:T(8,128)}, f32[32,256]{1,0:T(8,128)}, f32[32,256]{1,0:T(8,128)}, /*index=5*/f3...) custom-call(f32[8,32,256]{2,1,0:T(8,128)} %get-tuple-element.20.src, ...), custom_call_target="tpu_custom_call" | custom-call | tf_op jit(solution)/shard_map/split/pallas_call | solution.py:557

commit v3 on v2

--- a/solution.py
+++ b/solution.py
@@ -15,6 +15,7 @@
 SWEEPS = 2
 NEAR = (1, -1, 2, -2)
 FAR = 5
+LINK_ORDER = (4, 3, 5, 2, 6, 1, 7)
 N_SEMS = 360
 LANES = 128
 TOP = 32766.0
@@ -147,7 +148,7 @@
 
     def link_gather(buf):
         out = []
-        for d in range(1, n_link):
+        for d in LINK_ORDER:
             out.append(send(buf.at[0], buf.at[-d % n_link], link_dev(d)))
         return out
 
@@ -182,24 +183,18 @@
     def columns_send(s, h):
         g = refs.yg[s][h]
         terms = [dot_nn(g[row_slot[k]], refs.tiles_v[k]) for k in range(slots)]
-        parts, out, scale = refs.cpart[s][h], refs.cout[s][h], refs.cscale_out[s][h]
-        top = least
-        for o in range(n_link):
-            parts[o] = picked(col_at, terms, o)
-            top = lane_top(parts[o], top)
-        scale[...] = top * (1.0 / TOP)
-        inverse = wide(TOP / top)
+        out = refs.cout[s][h]
         copies = []
+        for o in LINK_ORDER + (0,):
+            out[o] = picked(col_at, terms, o)
+            if o:
+                copies.append(send(out.at[o], refs.cin[s][h].at[o], link_dev(o)))
+        return copies
+
+    def primal_update(s, h):
+        total = refs.cout[s][h][0]
         for o in range(1, n_link):
-            copies.append(send(scale, refs.cscale[s][h].at[o], link_dev(o)))
-            out[o] = fixed(parts[o], inverse)
-            copies.append(send(out.at[o], refs.cin[s][h].at[o], link_dev(o)))
-        return copies
-
-    def primal_update(s, h):
-        total = refs.cpart[s][h][0]
-        for o in range(1, n_link):
-            total = total + loose(refs.cin[s][h][o], refs.cscale[s][h][o])
+            total = total + refs.cin[s][h][o]
         linked = refs.wg[s][target_at]
         gradient = total - dot_nn(part(linked, h), refs.ltile_v[...])
         old = x[s, rows_of(h), :]
@@ -282,7 +277,7 @@
         scaled = term * wide(TOP / top)
         refs.lsum[s][...] = jnp.where(target_at == 0, 1.0, 0.0) * term
         copies = []
-        for o in range(1, n_link):
+        for o in LINK_ORDER:
             copies.append(send(refs.lscale_out[s], refs.lscale[s].at[o], link_dev(o)))
             out[o] = fixed(scaled, jnp.where(target_at == o, 1.0, 0.0))
             copies.append(send(out.at[o], refs.lin[s].at[o], link_dev(o)))
@@ -315,7 +310,7 @@
         return [send(buf.at[at], buf.at[at], d) for d in devs]
 
     region_devs = [region_dev(o) for o in range(1, n_region)]
-    link_devs = [link_dev(o) for o in range(1, n_link)]
+    link_devs = [link_dev(o) for o in LINK_ORDER]
 
     def z_spread(buf, value):
         buf[t] = value
@@ -346,8 +341,16 @@
         bar = 2.0 * z[s + 1] - z[s]
         w[s + 1] = jnp.maximum(w[s] + step_d * (refs.linkage_bound[...] - (bar - total)), 0.0)
 
+    stores = []
+
+    def store(i, value):
+        refs.result[i] = value
+        c = pltpu.make_async_copy(refs.result.at[i], out.at[i], refs.osem.at[i])
+        c.start()
+        stores.append(c)
+
     def average(mean, state, i):
-        out[i] = (weight * mean + state[1] + state[2]) / (weight + 2.0)
+        store(i, (weight * mean + state[1] + state[2]) / (weight + 2.0))
 
     ready = [duals_send(0, h) for h in range(HALVES)]
     w_copies = link_gather(refs.wg[0])
@@ -390,8 +393,8 @@
             directs[h] += rows_relay(s, h, relays[h])
         link_copies = linking_z(s, link_copies)
         if last:
-            out[0] = x[2]
-            out[1] = z[2]
+            store(0, x[2])
+            store(1, z[2])
             average(refs.primal_mean_v[...], x, 4)
             average(refs.capacity_mean_v[...], z, 5)
         for h in range(HALVES):
@@ -410,7 +413,7 @@
         return jnp.sum(jnp.where(on, jnp.broadcast_to(col, (scen, lanes)), 0.0), axis=0, keepdims=True)
 
     copies = z_spread(refs.mz, as_row(squares(x) + squares(y)))
-    out[2] = y[2]
+    store(2, y[2])
     average(refs.duals_mean_v[...], y, 6)
     z_relay(refs.lz[SWEEPS - 1], link_copies)
     z_relay(refs.mz, copies)
@@ -419,7 +422,7 @@
     copies = spread(refs.mreg, r, summed(refs.mz, n_tile), region_devs)
     linking_update(SWEEPS - 1, link_copies)
     moved = as_row(squares(z) + squares(w))
-    out[3] = w[2]
+    store(3, w[2])
     average(refs.linkage_mean_v[...], w, 7)
     finish(copies)
     copies = spread(refs.mlink, l, summed(refs.mreg, n_region) + moved, link_devs)
@@ -427,6 +430,8 @@
     moved_out[...] = summed(refs.mlink, n_link)
     for c in sent:
         c.wait_send()
+    for c in stores:
+        c.wait()
 
 
 def on_device(
@@ -481,6 +486,8 @@
         ssem=pltpu.SemaphoreType.DMA((N_SEMS,)),
         rsem=pltpu.SemaphoreType.DMA((N_SEMS,)),
         lsem=pltpu.SemaphoreType.DMA((11,)),
+        osem=pltpu.SemaphoreType.DMA((8,)),
+        result=pltpu.VMEM((8, scen, width), F32),
         tiles_v=pltpu.VMEM((slots, width, width), BF16),
         ltile_v=pltpu.VMEM((width, width), BF16),
         mz=pltpu.VMEM((n_tile, 1, 128), F32),
@@ -510,11 +517,8 @@
         lback=per_sweep((n_region, piece, width), F32),
         yg=per_half((n_tile, half, width), BF16),
         eg=per_half((n_link, half, width), BF16),
-        cpart=per_half((n_link, half, width), F32),
-        cout=per_half((n_link, half, width), I16),
-        cin=per_half((n_link, half, width), I16),
-        cscale=per_half((n_link, 1, LANES), F32),
-        cscale_out=per_half((1, LANES), F32),
+        cout=per_half((n_link, half, width), F32),
+        cin=per_half((n_link, half, width), F32),
         rpart=per_half((n_tile, half, width), F32),
         rout=per_half((5, 2, half, width), I16),
         rin=per_half((5, 2, half, width), I16),
@@ -535,7 +539,7 @@
         body,
         out_shape=(results, moved),
         in_specs=({k: v[1] for k, v in inputs.items()},),
-        out_specs=(vmem, vmem),
+        out_specs=(hbm, vmem),
         scratch_shapes=(scratch,),
         compiler_params=pltpu.CompilerParams(
             collective_id=0, has_side_effects=True, vmem_limit_bytes=VMEM_LIMIT

time: 106 us -> 106 us (level)
  no operation moved by 1% of the time
where the time goes in v3:
time: 106 us
  Pallas kernels  104 us (98%)
  between operations  1.95 us (2%)
    pallas_call x1, Pallas kernels, on_device(): pl.pallas_call(body, out_shape=(results, moved), in_specs=({k: v[1] for k...  102 us
    pallas_call x1, Pallas kernels, on_device(): pl.pallas_call(split, out_shape=[one] * 8 + [jax.ShapeDtypeStruct((1, sce...  2.22 us

profile of v3, /device:TPU:1, one launch (start us, length us, event | category | flops | bytes accessed | tf_op | source)
XLA Modules:
  0.0 105.8 jit_solution(9661262437333914099)
XLA Ops:
  1.9 101.6 %pdhg.1 = (f32[8,32,256]{2,1,0:T(8,128)}, f32[1,128]{1,0:T(1,128)}) custom-call(f32[1,256]{1,0:T(1,128)} %bitcast.12, f32[32,256]{1,0:T(8,128)} %ins__capacity_mean__.1, f32[32,256]{1,0:T(8,128)} %ins__capacity_now__.1, s32[1,1,8]{2,1,0:T(1,128)} %ins__cols__.1, f32[1,256]{1,0:T(1,128)} %bitcast.13, s32[1,1,1]{2,1,0:T(1,128)S(6)} %copy.31.ins__count__, ...), custom_call_target="tpu_custom_call" | custom-call | flops 80000000 | bytes 2000000 | tf_op jit(solution)/shard_map/pdhg/pallas_call | solution.py:538
  103.6 2.2 %split.1 = (f32[32,256]{1,0:T(8,128)}, f32[32,256]{1,0:T(8,128)}, f32[32,256]{1,0:T(8,128)}, f32[32,256]{1,0:T(8,128)}, f32[32,256]{1,0:T(8,128)}, /*index=5*/f3...) custom-call(f32[8,32,256]{2,1,0:T(8,128)} %get-tuple-element.20.src, ...), custom_call_target="tpu_custom_call" | custom-call | tf_op jit(solution)/shard_map/split/pallas_call | solution.py:561

commit v4 on v3

--- a/solution.py
+++ b/solution.py
@@ -13,7 +13,7 @@
 BF16 = jnp.bfloat16
 HALVES = 2
 SWEEPS = 2
-NEAR = (1, -1, 2, -2)
+NEAR = (2, -2, 1, -1)
 FAR = 5
 LINK_ORDER = (4, 3, 5, 2, 6, 1, 7)
 N_SEMS = 360
@@ -66,10 +66,14 @@
     barrier = pltpu.get_barrier_semaphore()
     for o in Z_PARTNERS:
         pl.semaphore_signal(barrier, inc=1, device_id=z_dev(o), device_id_type=MESH)
-    for o in range(1, n_link):
-        pl.semaphore_signal(barrier, inc=1, device_id=link_dev(o), device_id_type=MESH)
-    for o in range(1, n_region):
-        pl.semaphore_signal(barrier, inc=1, device_id=region_dev(o), device_id_type=MESH)
+    plane_devs = [
+        (lax.rem(r + i, n_region), t, lax.rem(l + j, n_link))
+        for i in range(n_region)
+        for j in LINK_ORDER + (0,)
+        if i or j
+    ]
+    for d in plane_devs:
+        pl.semaphore_signal(barrier, inc=1, device_id=d, device_id_type=MESH)
 
     def load(i, src, dst):
         c = pltpu.make_async_copy(src, dst, refs.lsem.at[i])
@@ -77,6 +81,12 @@
         return c
 
     duals_loads = [load(0, refs.duals_now, refs.duals_now_v), load(1, refs.duals_mean, refs.duals_mean_v)]
+    small_loads = [
+        load(11, refs.restart, refs.restart_v),
+        load(12, refs.mean_count, refs.mean_count_v),
+        load(13, refs.primal_step, refs.primal_step_v),
+        load(14, refs.dual_step, refs.dual_step_v),
+    ]
     linkage_loads = [load(2, refs.linkage_now, refs.linkage_now_v), load(3, refs.linkage_mean, refs.linkage_mean_v)]
     other_loads = [
         load(4, refs.tiles, refs.tiles_v),
@@ -86,6 +96,9 @@
         load(8, refs.primal_mean, refs.primal_mean_v),
         load(9, refs.capacity_now, refs.capacity_now_v),
         load(10, refs.capacity_mean, refs.capacity_mean_v),
+        load(15, refs.column_cost, refs.column_cost_v),
+        load(16, refs.capacity_cost, refs.capacity_cost_v),
+        load(17, refs.linkage_bound, refs.linkage_bound_v),
     ]
 
     eye = lax.broadcasted_iota(jnp.int32, (scen, scen), 0) == lax.broadcasted_iota(jnp.int32, (scen, scen), 1)
@@ -93,11 +106,13 @@
     def column(row):
         return jnp.sum(jnp.where(eye, jnp.broadcast_to(row, (scen, scen)), 0.0), axis=1, keepdims=True)
 
-    restart_row = refs.restart[...].astype(F32)
+    for c in small_loads:
+        c.wait()
+    restart_row = refs.restart_v[...].astype(F32)
     restarted = jnp.broadcast_to(column(restart_row), (scen, width)) == 1.0
-    weight = jnp.broadcast_to(column(refs.mean_count[...].astype(F32) * (1.0 - restart_row)), (scen, width))
-    step_p = jnp.broadcast_to(column(refs.primal_step[...]), (scen, width))
-    step_d = jnp.broadcast_to(column(refs.dual_step[...]), (scen, width))
+    weight = jnp.broadcast_to(column(refs.mean_count_v[...].astype(F32) * (1.0 - restart_row)), (scen, width))
+    step_p = jnp.broadcast_to(column(refs.primal_step_v[...]), (scen, width))
+    step_d = jnp.broadcast_to(column(refs.dual_step_v[...]), (scen, width))
 
     def part(value, h):
         return value[h * half : (h + 1) * half]
@@ -126,7 +141,7 @@
     w[0] = jnp.where(restarted, refs.linkage_mean_v[...], refs.linkage_now_v[...])
     refs.wg[0][0] = w[0].astype(BF16)
 
-    pl.semaphore_wait(barrier, len(Z_PARTNERS) + n_link - 1 + n_region - 1)
+    pl.semaphore_wait(barrier, len(Z_PARTNERS) + len(plane_devs))
 
     def duals_send(s, h):
         g = refs.yg[s][h]
@@ -138,8 +153,8 @@
 
     def duals_forward(s, h, out):
         g = refs.yg[s][h]
-        order = (-3, -2, -1, 1, 2) if h == 0 else (-2, -1, 1, 2)
-        back = (3, 2, 1, -1, -2) if h == 1 else (2, 1, -1, -2)
+        order = (-3, -2, 2, -1, 1) if h == 0 else (-2, 2, -1, 1)
+        back = (3, 2, -2, 1, -1) if h == 1 else (2, -2, 1, -1)
         for slot, moves in ((FAR, order), (n_tile - FAR, back)):
             out.pop(slot).wait_recv()
             for d in moves:
@@ -163,11 +178,18 @@
             total = one if total is None else total + one
         return total
 
-    def lane_top(value, top):
+    def folded(value, top):
         value = jnp.abs(value)
         for i in range(0, width, LANES):
-            top = jnp.maximum(top, jnp.max(value[:, i : i + LANES], axis=0, keepdims=True))
+            lanes = value[:, i : i + LANES]
+            top = lanes if top is None else jnp.maximum(top, lanes)
         return top
+
+    def lane_top(values):
+        top = None
+        for value in values:
+            top = folded(value, top)
+        return jnp.maximum(jnp.max(top, axis=0, keepdims=True), 1e-30)
 
     def wide(row):
         return jnp.concatenate([row] * (width // LANES), axis=1)
@@ -177,8 +199,6 @@
 
     def loose(value, scale):
         return value.astype(jnp.int32).astype(F32) * wide(scale)
-
-    least = jnp.full((1, LANES), 1e-30, F32)
 
     def columns_send(s, h):
         g = refs.yg[s][h]
@@ -198,7 +218,7 @@
         linked = refs.wg[s][target_at]
         gradient = total - dot_nn(part(linked, h), refs.ltile_v[...])
         old = x[s, rows_of(h), :]
-        new = jnp.maximum(old - part(step_p, h) * (refs.column_cost[...] - gradient), 0.0)
+        new = jnp.maximum(old - part(step_p, h) * (refs.column_cost_v[...] - gradient), 0.0)
         x[s + 1, rows_of(h), :] = new
         extrap = (2.0 * new - old).astype(BF16)
         refs.eg[s][h][0] = extrap
@@ -207,23 +227,23 @@
         g = refs.eg[s][h]
         terms = [dot_nt(g[col_slot[k]], refs.tiles_v[k]) for k in range(slots)]
         parts, out, near, scale = refs.rpart[s][h], refs.rout[s][h], refs.rnear[s][h], refs.rscale_out[s][h]
-        top = least
+        top = None
         for o in range(n_tile):
-            parts[o] = picked(row_at, terms, o)
-            top = lane_top(parts[o], top)
+            one = picked(row_at, terms, o)
+            parts[o] = one
+            top = folded(one, top)
+        top = jnp.maximum(jnp.max(top, axis=0, keepdims=True), 1e-30)
         scale[...] = top * (1.0 / TOP)
         inverse = wide(TOP / top)
         third = 3 if h == 0 else -3
-        copies = []
+        copies = [send(scale, refs.rscale[s][h].at[4], z_dev(-third))]
+        out[4, 0] = fixed(parts[n_tile // 2], inverse)
+        copies.append(send(out.at[4, 0], refs.rin[s][h].at[4, 0], z_dev(-third)))
         for i, e in enumerate(NEAR):
             copies.append(send(scale, refs.rscale[s][h].at[i], z_dev(-e)))
             out[i, 0] = fixed(parts[(-e - FAR) % n_tile], inverse)
             out[i, 1] = fixed(parts[(-e + FAR) % n_tile], inverse)
             copies.append(send(out.at[i], refs.rin[s][h].at[i], z_dev(-e)))
-            if i == 0:
-                copies.append(send(scale, refs.rscale[s][h].at[4], z_dev(-third)))
-                out[4, 0] = fixed(parts[n_tile // 2], inverse)
-                copies.append(send(out.at[4, 0], refs.rin[s][h].at[4, 0], z_dev(-third)))
         for i, e in enumerate(NEAR):
             near[i] = fixed(parts[-e % n_tile], inverse)
         return copies
@@ -236,7 +256,7 @@
     def rows_relay(s, h, copies):
         finish(copies)
         got, parts, scale = refs.rin[s][h], refs.rpart[s][h], refs.rscale[s][h]
-        totals, top = [], least
+        totals = []
         for j in range(2):
             total = parts[FAR if j else n_tile - FAR]
             for i in range(4):
@@ -244,7 +264,7 @@
             if j == h:
                 total = total + loose(got[4, 0], scale[4])
             totals.append(total)
-            top = lane_top(total, top)
+        top = lane_top(totals)
         refs.fscale_out[s][h][...] = top * (1.0 / TOP)
         inverse = wide(TOP / top)
         result = []
@@ -272,7 +292,7 @@
         out = refs.lout[s]
         e = jnp.concatenate([refs.eg[s][h][0] for h in range(HALVES)], axis=0)
         term = dot_nt(e, refs.ltile_v[...])
-        top = lane_top(term, least)
+        top = lane_top([term])
         refs.lscale_out[s][...] = top * (1.0 / TOP)
         scaled = term * wide(TOP / top)
         refs.lsum[s][...] = jnp.where(target_at == 0, 1.0, 0.0) * term
@@ -317,7 +337,7 @@
         return {d: send(buf.at[t], buf.at[t], z_dev(-d)) for d in (FAR, -FAR) + NEAR}
 
     def z_relay(buf, out):
-        for d, moves in ((FAR, (-3, -2, -1, 1, 2)), (-FAR, (2, 1, -1, -2))):
+        for d, moves in ((FAR, (-3, -2, 2, -1, 1)), (-FAR, (2, -2, 1, -1))):
             out.pop(d).wait_recv()
             at = lax.rem(t + (d + n_tile), n_tile)
             for m in moves:
@@ -332,14 +352,14 @@
         return spread(refs.lback[s], r, summed(refs.lz[s], n_tile), region_devs)
 
     def capacity_update(s):
-        z[s + 1] = jnp.maximum(z[s] - step_p * (refs.capacity_cost[...] - w[s]), 0.0)
+        z[s + 1] = jnp.maximum(z[s] - step_p * (refs.capacity_cost_v[...] - w[s]), 0.0)
 
     def linking_update(s, copies):
         finish(copies)
         back = refs.lback[s]
         total = jnp.concatenate([back[i] for i in range(n_region)], axis=0)
         bar = 2.0 * z[s + 1] - z[s]
-        w[s + 1] = jnp.maximum(w[s] + step_d * (refs.linkage_bound[...] - (bar - total)), 0.0)
+        w[s + 1] = jnp.maximum(w[s] + step_d * (refs.linkage_bound_v[...] - (bar - total)), 0.0)
 
     stores = []
 
@@ -366,14 +386,14 @@
             duals_forward(s, h, ready[h])
         if s:
             link_copies = linking_back(s - 1, link_copies)
+        if s:
+            linking_update(s - 1, link_copies)
+            refs.wg[s][0] = w[s].astype(BF16)
+            w_copies = link_gather(refs.wg[s])
         columns = []
         for h in range(HALVES):
             finish(ready[h].values())
             columns.append(columns_send(s, h))
-        if s:
-            linking_update(s - 1, link_copies)
-            refs.wg[s][0] = w[s].astype(BF16)
-            w_copies = link_gather(refs.wg[s])
         capacity_update(s)
         finish(w_copies)
         gathers = []
@@ -391,7 +411,8 @@
         link_copies = linking_region(s, link_copies)
         for h in range(HALVES):
             directs[h] += rows_relay(s, h, relays[h])
-        link_copies = linking_z(s, link_copies)
+            if h == 0:
+                link_copies = linking_z(s, link_copies)
         if last:
             store(0, x[2])
             store(1, z[2])
@@ -418,16 +439,14 @@
     z_relay(refs.lz[SWEEPS - 1], link_copies)
     z_relay(refs.mz, copies)
     link_copies = linking_back(SWEEPS - 1, link_copies)
+    linking_update(SWEEPS - 1, link_copies)
+    moved = jnp.where(r == 0, 1.0, 0.0) * as_row(squares(z) + squares(w))
     finish(copies.values())
-    copies = spread(refs.mreg, r, summed(refs.mz, n_tile), region_devs)
-    linking_update(SWEEPS - 1, link_copies)
-    moved = as_row(squares(z) + squares(w))
+    copies = spread(refs.mplane, r * n_link + l, summed(refs.mz, n_tile) + moved, plane_devs)
     store(3, w[2])
     average(refs.linkage_mean_v[...], w, 7)
     finish(copies)
-    copies = spread(refs.mlink, l, summed(refs.mreg, n_region) + moved, link_devs)
-    finish(copies)
-    moved_out[...] = summed(refs.mlink, n_link)
+    moved_out[...] = summed(refs.mplane, n_region * n_link)
     for c in sent:
         c.wait_send()
     for c in stores:
@@ -453,13 +472,13 @@
         cols=(tile_col, smem),
         count=(tile_count, smem),
         target=(linkage_block, smem),
-        restart=(restart.reshape(1, scen), vmem),
-        mean_count=(mean_count.reshape(1, scen), vmem),
-        primal_step=(primal_step.reshape(1, scen), vmem),
-        dual_step=(dual_step.reshape(1, scen), vmem),
-        column_cost=(column_cost.reshape(1, width), vmem),
-        capacity_cost=(capacity_cost.reshape(1, width), vmem),
-        linkage_bound=(linkage_bound.reshape(1, width), vmem),
+        restart=(restart.reshape(1, scen), hbm),
+        mean_count=(mean_count.reshape(1, scen), hbm),
+        primal_step=(primal_step.reshape(1, scen), hbm),
+        dual_step=(dual_step.reshape(1, scen), hbm),
+        column_cost=(column_cost.reshape(1, width), hbm),
+        capacity_cost=(capacity_cost.reshape(1, width), hbm),
+        linkage_bound=(linkage_bound.reshape(1, width), hbm),
         tiles=(tiles.reshape(slots, width, width), hbm),
         ltile=(linkage_tiles.reshape(width, width), hbm),
         demand=(demand, hbm),
@@ -485,14 +504,20 @@
     scratch = dict(
         ssem=pltpu.SemaphoreType.DMA((N_SEMS,)),
         rsem=pltpu.SemaphoreType.DMA((N_SEMS,)),
-        lsem=pltpu.SemaphoreType.DMA((11,)),
+        lsem=pltpu.SemaphoreType.DMA((18,)),
         osem=pltpu.SemaphoreType.DMA((8,)),
         result=pltpu.VMEM((8, scen, width), F32),
         tiles_v=pltpu.VMEM((slots, width, width), BF16),
         ltile_v=pltpu.VMEM((width, width), BF16),
         mz=pltpu.VMEM((n_tile, 1, 128), F32),
-        mreg=pltpu.VMEM((n_region, 1, 128), F32),
-        mlink=pltpu.VMEM((n_link, 1, 128), F32),
+        mplane=pltpu.VMEM((n_region * n_link, 1, 128), F32),
+        restart_v=pltpu.VMEM((1, scen), jnp.int32),
+        mean_count_v=pltpu.VMEM((1, scen), jnp.int32),
+        primal_step_v=pltpu.VMEM((1, scen), F32),
+        dual_step_v=pltpu.VMEM((1, scen), F32),
+        column_cost_v=pltpu.VMEM((1, width), F32),
+        capacity_cost_v=pltpu.VMEM((1, width), F32),
+        linkage_bound_v=pltpu.VMEM((1, width), F32),
         duals_now_v=block,
         duals_mean_v=block,
         linkage_now_v=block,

time: 106 us -> 103 us (0.972)
  Pallas kernels: 104 us -> 101 us
    pallas_call x1, Pallas kernels: 102 us -> 98.9 us  [on_device(): pl.pallas_call(body, out_shape=(results, moved), in_specs=({k: v[1] for k...]
where the time goes in v4:
time: 103 us
  Pallas kernels  101 us (98%)
  between operations  1.95 us (2%)
    pallas_call x1, Pallas kernels, on_device(): pl.pallas_call(body, out_shape=(results, moved), in_specs=({k: v[1] for k...  98.9 us
    pallas_call x1, Pallas kernels, on_device(): pl.pallas_call(split, out_shape=[one] * 8 + [jax.ShapeDtypeStruct((1, sce...  2.22 us

profile of v4, /device:TPU:1, one launch (start us, length us, event | category | flops | bytes accessed | tf_op | source)
XLA Modules:
  0.0 103.1 jit_solution(9245183732826708132)
XLA Ops:
  1.9 98.9 %pdhg.1 = (f32[8,32,256]{2,1,0:T(8,128)}, f32[1,128]{1,0:T(1,128)}) custom-call(f32[1,256]{1,0:T(1,128)} %bitcast.12, f32[32,256]{1,0:T(8,128)} %ins__capacity_mean__.1, f32[32,256]{1,0:T(8,128)} %ins__capacity_now__.1, s32[1,1,8]{2,1,0:T(1,128)} %ins__cols__.1, f32[1,256]{1,0:T(1,128)} %bitcast.13, s32[1,1,1]{2,1,0:T(1,128)S(6)} %copy.31.ins__count__, ...), custom_call_target="tpu_custom_call" | custom-call | flops 80000000 | bytes 2000000 | tf_op jit(solution)/shard_map/pdhg/pallas_call | solution.py:563
  100.9 2.2 %split.1 = (f32[32,256]{1,0:T(8,128)}, f32[32,256]{1,0:T(8,128)}, f32[32,256]{1,0:T(8,128)}, f32[32,256]{1,0:T(8,128)}, f32[32,256]{1,0:T(8,128)}, /*index=5*/f3...) custom-call(f32[8,32,256]{2,1,0:T(8,128)} %get-tuple-element.20.src, ...), custom_call_target="tpu_custom_call" | custom-call | tf_op jit(solution)/shard_map/split/pallas_call | solution.py:586
